TPU v7x, 32 devices: a whole 2x2x4 slice. The times are simulated.
32 devices in a mesh: groups: 2 (over y), seq: 4 (over z), head: 2 (over x), rep: 2 (over core).
Axes of the slice: x: 2, y: 2, z: 4, core: 2. Of those that a mesh axis runs over, the one named last changes fastest.
Arguments:
- queries: bfloat16 [8192, 2048], P(('groups', 'seq'), ('head', 'rep')), parts along dimension 0, may hold values from -8 to 8
- keys_values: bfloat16 [2, 8192, 2048], P(None, ('groups', 'seq'), ('head', 'rep')), parts along dimension 1, may hold values from -8 to 8
- pack_pos: int32 [1024], P('groups'), parts along dimension 0, may hold values from 0 to 4095
- bounds: int32 [2, 8192], P(None, ('groups', 'seq')), parts along dimension 1, may hold values from 0 to 4096, as said below
- radius: int32 [32], P(('head', 'rep')), may hold values from 128 to 512, as said below
- pack_proj: bfloat16 [2, 2048, 2048], P(None, None, ('head', 'rep')), may hold values from -0.5 to 0.5
Outputs:
- mixed: bfloat16 [8192, 2048], P(('groups', 'seq'), ('head', 'rep')), parts along dimension 0
There are 2 independent parts, one for each index of `groups`. A program takes and returns all parts, laid end to end along the dimension named above; an argument that names none is the same for every part. Nothing has to cross between parts.
Inputs may be any that keep to these rules, and one draw needn't show every extreme that they name: bounds[0, s] and bounds[1, s] are the first position and the end (exclusive) of the document of token s; the 8 documents are contiguous and tile the sequence. Some head has radius exactly 512.
All inputs are finite; a program needn't handle non-finite values.
Results may differ from a plain program's by a relative error of at most 0.012.
Values may be sent and summed in bfloat16 or wider, within the bound.
A program may use at most 128 MiB of HBM per device.

v0:
```python
import functools
import math

import jax
import jax.numpy as jnp
from jax import lax
from jax.experimental import pallas as pl
from jax.experimental.pallas import tpu as pltpu
from jax.sharding import PartitionSpec as P

HEAD_DIM = 64
PACK = 512
RADIUS = 512
PAIR = 2 * HEAD_DIM
ROWS = 256
LOG2E = 1.4426950408889634
FACTOR = LOG2E / math.sqrt(HEAD_DIM)
LOW = -1e30
VMEM = 48 * 1024 * 1024


def lane_half(rows):
    return lax.broadcasted_iota(jnp.int32, (rows, PAIR), 1) // HEAD_DIM


def dot_t(a, b):
    return lax.dot_general(a, b, (((1,), (1,)), ((), ())), preferred_element_type=jnp.float32)


def only_head(x, h):
    return jnp.where(lane_half(x.shape[0]) == h, x, jnp.zeros_like(x))


def with_ones(x, h):
    return jnp.where(lane_half(x.shape[0]) == h, x, jnp.ones_like(x))


def softmax_dot(scores, values):
    top = jnp.max(scores, axis=1, keepdims=True)
    weights = jnp.exp2((scores - top) * FACTOR)
    acc = jnp.dot(weights.astype(jnp.bfloat16), values, preferred_element_type=jnp.float32)
    return top * FACTOR, acc


def merge_heads(tops, accs):
    half = lane_half(accs[0].shape[0])
    summed = jnp.where(half == 0, accs[0], accs[1])
    total = pltpu.roll(jnp.where(half == 0, accs[1], accs[0]), HEAD_DIM, 1)
    top = jnp.where(half == 0, tops[0], tops[1])
    return summed, total, top


def pack_kernel(kv_ref, *refs):
    *shares, out_ref, queries, lse_ref = refs
    pair = pl.program_id(0)
    columns = pl.ds(pl.multiple_of(pair * PAIR, PAIR), PAIR)
    for j, ref in enumerate(shares):
        queries[pl.ds(j * ref.shape[0], ref.shape[0]), :] = ref[...]
    keys = kv_ref[0]
    values = [with_ones(kv_ref[1], h) for h in range(2)]
    for r in range(0, queries.shape[0], ROWS):
        rows = pl.ds(r, ROWS)
        q = queries[rows, :]
        tops, accs = [], []
        for h in range(2):
            top, acc = softmax_dot(dot_t(only_head(q, h), keys), values[h])
            tops.append(top)
            accs.append(acc)
        summed, total, top = merge_heads(tops, accs)
        out_ref[rows, columns] = (summed / total).astype(jnp.bfloat16)
        lse = top + jnp.log2(total)
        lane = lax.broadcasted_iota(jnp.int32, (ROWS, 128), 1)
        for h in range(2):
            column = lse[:, h * HEAD_DIM : h * HEAD_DIM + 1]
            lse_ref[rows, :] = jnp.where(lane == 2 * pair + h, column, lse_ref[rows, :])

    @pl.when(pair == pl.num_programs(0) - 1)
    def _():
        lse = lse_ref[...]
        high = lse.astype(jnp.bfloat16).astype(jnp.float32)
        middle = (lse - high).astype(jnp.bfloat16).astype(jnp.float32)
        low = lse - high - middle
        lane = lax.broadcasted_iota(jnp.int32, lse.shape, 1)
        terms = jnp.where(lane < 64, pltpu.roll(middle, 32, 1), pltpu.roll(low, 64, 1))
        terms = jnp.where(lane < 32, high, terms)
        out_ref[:, out_ref.shape[1] - 128 :] = terms.astype(jnp.bfloat16)


def pack_attention(shares, keys_values):
    share, width = shares[0].shape
    rows = share * len(shares)
    tokens = keys_values.shape[1]
    return pl.pallas_call(
        pack_kernel,
        grid=(width // PAIR,),
        in_specs=[pl.BlockSpec((2, tokens, PAIR), lambda i: (0, 0, i))]
        + [pl.BlockSpec((share, PAIR), lambda i: (0, i))] * len(shares),
        out_specs=pl.BlockSpec((rows, width + 128), lambda i: (0, 0)),
        out_shape=jax.ShapeDtypeStruct((rows, width + 128), jnp.bfloat16),
        scratch_shapes=[
            pltpu.VMEM((rows, PAIR), jnp.bfloat16),
            pltpu.VMEM((rows, 128), jnp.float32),
        ],
        compiler_params=pltpu.CompilerParams(vmem_limit_bytes=VMEM),
        cost_estimate=pl.CostEstimate(
            flops=16 * rows * tokens * width,
            bytes_accessed=4 * tokens * width + 8 * rows * width,
            transcendentals=rows * tokens * width // HEAD_DIM,
        ),
        name="pack_attention",
    )(keys_values, *shares)


def combine_kernel(*refs):
    *parts, out_ref = refs
    rows, width = out_ref.shape
    held = [ref[:, width:].astype(jnp.float32) for ref in parts]
    held = [x + pltpu.roll(x, 96, 1) + pltpu.roll(x, 64, 1) for x in held]
    highest = functools.reduce(jnp.maximum, held)
    weights = [jnp.exp2(x - highest) for x in held]
    total = sum(weights)
    weights = [w / total for w in weights]
    half = lane_half(rows)
    for pair in range(width // PAIR):
        columns = pl.ds(pair * PAIR, PAIR)
        summed = jnp.zeros((rows, PAIR), jnp.float32)
        for ref, w in zip(parts, weights):
            one, two = (w[:, 2 * pair + h : 2 * pair + h + 1] for h in range(2))
            summed += ref[:, columns].astype(jnp.float32) * jnp.where(half == 0, one, two)
        out_ref[:, columns] = summed.astype(jnp.bfloat16)


def combine(parts):
    rows, width = parts[0].shape
    return pl.pallas_call(
        combine_kernel,
        out_shape=jax.ShapeDtypeStruct((rows, width - 128), jnp.bfloat16),
        name="combine",
    )(*parts)


def window_kernel(
    first_pair, radius_ref, bounds_ref, q_ref, own_ref, left_ref, right_ref, limits_ref, *rest
):
    out_ref, lse_ref, keys, values, accs, tops = rest[-6:]
    tokens = q_ref.shape[0]
    pair = first_pair + pl.program_id(0)
    for at, ref in ((0, left_ref), (RADIUS, own_ref), (RADIUS + tokens, right_ref)):
        span = pl.ds(at, ref.shape[1])
        keys[span, :] = ref[0]
        for h in range(2):
            values[h, span, :] = with_ones(ref[1], h)

    def block(b, carry):
        first = pl.multiple_of(b * ROWS, ROWS)
        rows = pl.ds(first, ROWS)
        q = q_ref[rows, :]
        position = first + RADIUS + lax.broadcasted_iota(jnp.int32, (ROWS, 1), 0)
        lower = limits_ref[rows, 0:1]
        upper = limits_ref[rows, 1:2]
        for h in range(2):
            radius = radius_ref[2 * pair + h]
            low = jnp.maximum(lower, position - radius)
            high = jnp.minimum(upper, position + radius + 1)
            start = jnp.maximum(bounds_ref[first], first + RADIUS - radius)
            start = jnp.maximum(start, 0) // 128 * 128
            end = jnp.minimum(bounds_ref[tokens + first + ROWS - 1], first + RADIUS + ROWS + radius)
            need = end - start
            masked_q = only_head(q, h)

            def body(width):
                at = pl.multiple_of(jnp.minimum(start, tokens + 2 * RADIUS - width), 128)
                scores = dot_t(masked_q, keys[pl.ds(at, width), :])
                spot = lax.broadcasted_iota(jnp.int32, (ROWS, width), 1)
                allowed = (spot >= low - at) & (spot < high - at)
                top, acc = softmax_dot(
                    jnp.where(allowed, scores, LOW), values[h, pl.ds(at, width), :]
                )
                accs[h] = acc
                tops[h] = jnp.broadcast_to(top, (ROWS, PAIR))

            widest = ROWS + 2 * RADIUS
            widths = [w for w in (512, 640, 768, 896, 1024, 1152) if w < widest] + [widest]
            for index, width in enumerate(widths):
                fits = need <= width if width < widest else need > widths[index - 1]
                if 0 < index and width < widest:
                    fits = fits & (need > widths[index - 1])
                pl.when(fits)(functools.partial(body, width))
        summed, total, top = merge_heads([tops[0], tops[1]], [accs[0], accs[1]])
        out_ref[rows, :] = summed / total
        lse_ref[rows, :] = top + jnp.log2(total)
        return carry

    lax.fori_loop(0, tokens // ROWS, block, 0)


def window_attention(queries, keys_values, left, right, limits, radius, pairs, done):
    tokens, width = queries.shape
    cost = tokens * (ROWS + 2 * RADIUS)
    spec = lambda shape: pl.BlockSpec(shape, lambda i, *_: (0,) * (len(shape) - 1) + (i + pairs[0],))
    return pl.pallas_call(
        functools.partial(window_kernel, pairs[0]),
        grid_spec=pltpu.PrefetchScalarGridSpec(
            num_scalar_prefetch=2,
            grid=(pairs[1] - pairs[0],),
            in_specs=[
                spec((tokens, PAIR)),
                spec((2, tokens, PAIR)),
                spec((2, RADIUS, PAIR)),
                spec((2, RADIUS, PAIR)),
                pl.BlockSpec((tokens, 2), lambda i, *_: (0, 0)),
            ]
            + [pl.BlockSpec(memory_space=pl.ANY)] * len(done),
            out_specs=[spec((tokens, PAIR))] * 2,
            scratch_shapes=[
                pltpu.VMEM((tokens + 2 * RADIUS, PAIR), jnp.bfloat16),
                pltpu.VMEM((2, tokens + 2 * RADIUS, PAIR), jnp.bfloat16),
                pltpu.VMEM((2, ROWS, PAIR), jnp.float32),
                pltpu.VMEM((2, ROWS, PAIR), jnp.float32),
            ],
        ),
        out_shape=[jax.ShapeDtypeStruct((tokens, width), jnp.float32)] * 2,
        input_output_aliases={7 + i: i for i in range(len(done))},
        compiler_params=pltpu.CompilerParams(vmem_limit_bytes=VMEM),
        cost_estimate=pl.CostEstimate(
            flops=16 * cost * PAIR * (pairs[1] - pairs[0]),
            bytes_accessed=20 * tokens * PAIR * (pairs[1] - pairs[0]),
            transcendentals=2 * cost * (pairs[1] - pairs[0]),
        ),
        name="window_attention",
    )(radius, limits.reshape(-1), queries, keys_values, left, right, limits.T, *done)


def final_kernel(q_ref, part_ref, lse_ref, *refs):
    *shares, out_ref, pack = refs
    for j, ref in enumerate(shares):
        pack[:, pl.ds(j * ref.shape[1], ref.shape[1]), :] = ref[...]
    keys = pack[0]
    values = [with_ones(pack[1], h) for h in range(2)]
    for r in range(0, q_ref.shape[0], ROWS):
        rows = pl.ds(r, ROWS)
        q = q_ref[rows, :]
        tops, accs = [], []
        for h in range(2):
            top, acc = softmax_dot(dot_t(only_head(q, h), keys), values[h])
            tops.append(top)
            accs.append(acc)
        summed, total, top = merge_heads(tops, accs)
        other = lse_ref[rows, :]
        highest = jnp.maximum(top, other)
        mine = jnp.exp2(top - highest)
        theirs = jnp.exp2(other - highest)
        out_ref[rows, :] = (
            (summed * mine + part_ref[rows, :] * theirs) / (total * mine + theirs)
        ).astype(jnp.bfloat16)


def final_attention(queries, shares, part, lse):
    tokens, width = queries.shape
    spec = pl.BlockSpec((tokens, PAIR), lambda i: (0, i))
    return pl.pallas_call(
        final_kernel,
        grid=(width // PAIR,),
        in_specs=[spec] * 3
        + [pl.BlockSpec((2, x.shape[1], PAIR), lambda i: (0, 0, i)) for x in shares],
        out_specs=spec,
        scratch_shapes=[pltpu.VMEM((2, PACK, PAIR), jnp.bfloat16)],
        out_shape=jax.ShapeDtypeStruct((tokens, width), jnp.bfloat16),
        compiler_params=pltpu.CompilerParams(vmem_limit_bytes=VMEM),
        cost_estimate=pl.CostEstimate(
            flops=16 * tokens * PACK * width,
            bytes_accessed=12 * tokens * width,
            transcendentals=tokens * PACK * width // HEAD_DIM,
        ),
        name="final_attention",
    )(queries, part, lse, *shares)


def project_kernel(order_ref, part_ref, proj_ref, out_ref, acc):
    step = pl.program_id(0)

    @pl.when(step == 0)
    def _():
        acc[...] = jnp.zeros_like(acc)

    for which in range(2):
        acc[which] += jnp.dot(part_ref[0], proj_ref[which], preferred_element_type=jnp.float32)

    @pl.when(step == pl.num_programs(0) - 1)
    def _():
        out_ref[...] = acc[...].astype(jnp.bfloat16)


def project(order, parts, pack_proj):
    count, rows, width = parts.shape
    columns = pack_proj.shape[2]
    return pl.pallas_call(
        project_kernel,
        grid_spec=pltpu.PrefetchScalarGridSpec(
            num_scalar_prefetch=1,
            grid=(count,),
            in_specs=[
                pl.BlockSpec((1, rows, width), lambda i, order: (i, 0, 0)),
                pl.BlockSpec((2, width, columns), lambda i, order: (0, order[i], 0)),
            ],
            out_specs=pl.BlockSpec((2, rows, columns), lambda i, order: (0, 0, 0)),
            scratch_shapes=[pltpu.VMEM((2, rows, columns), jnp.float32)],
        ),
        out_shape=jax.ShapeDtypeStruct((2, rows, columns), jnp.bfloat16),
        compiler_params=pltpu.CompilerParams(vmem_limit_bytes=VMEM),
        name="project",
    )(order, parts, pack_proj)


def shifted(x, axis, count, shift):
    return lax.ppermute(x, axis, [(i, (i + shift) % count) for i in range(count)])


def shards(queries, keys_values, pack_pos, bounds, radius, pack_proj):
    tokens, width = queries.shape
    count = lax.axis_size("seq")
    share = PACK // count
    me = lax.axis_index("seq")
    first_pos = me * tokens

    ahead = (me + jnp.arange(count, dtype=jnp.int32)) % count
    local = pack_pos.reshape(count, share)[ahead].reshape(-1) - first_pos
    selector = (local[:, None] == jnp.arange(tokens, dtype=jnp.int32)[None, :]).astype(jnp.bfloat16)
    picked = jnp.dot(selector, queries, preferred_element_type=jnp.float32).astype(jnp.bfloat16)
    picked = picked.reshape(count, share, width)
    mine = picked[0]
    for s in range(1, count):
        mine = mine + shifted(picked[s], "seq", count, s)
    pack_query = [mine] + [shifted(mine, "seq", count, s) for s in range(1, count)]

    ends = count - 1
    tail, head = keys_values[:, tokens - RADIUS :], keys_values[:, :RADIUS]
    pack_query, tail, head = lax.optimization_barrier((pack_query, tail, head))
    left = lax.ppermute(tail, "seq", [(i, i + 1) for i in range(ends)])
    right = lax.ppermute(head, "seq", [(i + 1, i) for i in range(ends)])

    limits = bounds - (first_pos - RADIUS)
    pairs = width // PAIR
    edges = [0, 0, pairs // 4, pairs]
    window = ()

    def windowed(stage, after, beside):
        nonlocal window
        if edges[stage] == edges[stage + 1]:
            return beside
        held, _ = lax.optimization_barrier((radius, after))
        window = window_attention(
            queries, keys_values, left, right, limits, held, edges[stage : stage + 2], window
        )
        *window, beside = lax.optimization_barrier((*window, beside))
        return beside

    part = pack_attention(pack_query, keys_values).reshape(count, share, width + 128)
    parts = [part[0]] + [shifted(part[count - s], "seq", count, s) for s in range(1, count)]
    packed = combine(windowed(0, part, parts))

    axes = ("head", "rep")
    sides = lax.axis_size("head") * lax.axis_size("rep")
    here = lax.axis_index("head") * lax.axis_size("rep") + lax.axis_index("rep")
    gathered = [packed] + [shifted(packed, axes, sides, s) for s in range(1, sides)]
    gathered = jnp.stack(windowed(1, packed, gathered))
    order = (here - jnp.arange(sides, dtype=jnp.int32)) % sides
    pack_share = project(order, gathered, pack_proj)
    shares = [pack_share] + [shifted(pack_share, "seq", count, s) for s in range(1, count)]
    shares = windowed(2, pack_share, shares)
    return final_attention(queries, shares, *window)


def solution(mesh):
    return jax.shard_map(
        shards,
        mesh=mesh,
        in_specs=(
            P(("groups", "seq"), ("head", "rep")),
            P(None, ("groups", "seq"), ("head", "rep")),
            P("groups"),
            P(None, ("groups", "seq")),
            P(("head", "rep")),
            P(None, None, ("head", "rep")),
        ),
        out_specs=P(("groups", "seq"), ("head", "rep")),
        check_vma=False,
    )
```

profile of v0, /device:TPU:18, one launch (start us, length us, event | category | flops | bytes accessed | tf_op | source)
XLA Modules:
  0.0 137.3 jit_solution(13384009310260334037)
XLA Ops:
  0.0 0.7 copy-done
  0.7 0.6 gather_fusion
  1.3 2.1 %fusion.1 = bf16[512,512]{1,0:T(8,128)(2,1)S(1)} fusion(bf16[1024,512]{1,0:T(8,128)(2,1)} %q_ref.5, s32[512]{0:T(512)S(1)} %subtract_bitcast_fusion), kind=kOutput, calls=%fused_computation.3 | convolution fusion | flops 537657344 | bytes 1574912 | tf_op jit(solution)/shard_map/dot_general | solution.py:329
  3.4 1.6 %collective-permute-start = (bf16[128,512]{1,0:T(8,128)(2,1)S(1)}, bf16[128,512]{1,0:T(8,128)(2,1)S(1)}, u32[]{:S(2)}, u32[]{:S(2)}) collective-permute-start(bf16[128,512]{1,0:T(8,128)(2,1)S(1)} %get-tuple-element.59), channel_id=1, source_target_pairs={{0,4},{4,8},{8,12},{12,0},{1,5},{5,9},{9,13},{13,1},{2,6},{6,10},{... | collective-permute-start | bytes 393224 | tf_op jit(solution)/shard_map/ppermute | solution.py:316
  5.1 0.5 collective-permute-start.2
  5.5 2.1 %collective-permute-start.1 = (bf16[128,512]{1,0:T(8,128)(2,1)S(1)}, bf16[128,512]{1,0:T(8,128)(2,1)S(1)}, u32[]{:S(2)}, u32[]{:S(2)}) collective-permute-start(bf16[128,512]{1,0:T(8,128)(2,1)S(1)} %get-tuple-element.61), channel_id=1, source_target_pairs={{0,8},{4,12},{8,0},{12,4},{1,9},{5,13},{9,1},{13,5},{2,10},{6,14},... | collective-permute-start | bytes 393224 | tf_op jit(solution)/shard_map/ppermute | solution.py:316
  7.6 7.2 %collective-permute-done = bf16[128,512]{1,0:T(8,128)(2,1)S(1)} collective-permute-done((bf16[128,512]{1,0:T(8,128)(2,1)S(1)}, bf16[128,512]{1,0:T(8,128)(2,1)S(1)}, u32[]{:S(2)}, u32[]{:S(2)}) %collective-permute-start) | collective-permute-done | bytes 131104 | tf_op jit(solution)/shard_map/ppermute | solution.py:316
  14.9 1.1 collective-permute-done.1
  16.0 0.8 collective-permute-start.5
  16.8 4.3 %collective-permute-start.4 = (bf16[128,512]{1,0:T(8,128)(2,1)S(1)}, bf16[128,512]{1,0:T(8,128)(2,1)S(1)}, u32[]{:S(2)}, u32[]{:S(2)}) collective-permute-start(bf16[128,512]{1,0:T(8,128)(2,1)S(1)} %fusion.4.refs_0_), channel_id=1, source_target_pairs={{0,8},{4,12},{8,0},{12,4},{1,9},{5,13},{9,1},{13,5},{2,10},{6,14},... | collective-permute-start | bytes 393224 | tf_op jit(solution)/shard_map/ppermute | solution.py:316
  21.5 1.5 %fusion.8 = (bf16[2,512,512]{2,1,0:T(8,128)(2,1)}, bf16[2,512,512]{2,1,0:T(8,128)(2,1)}) fusion(bf16[2,1024,512]{2,1,0:T(8,128)(2,1)S(1)} %copy-done.2), kind=kLoop, calls=%fused_computation.23 | loop fusion | bytes 4194304 | tf_op jit(solution)/shard_map/slice | solution.py:337
  22.9 1.0 copy.12
  24.0 4.9 %collective-permute-done.4.refs_2_ = bf16[128,512]{1,0:T(8,128)(2,1)S(1)} collective-permute-done((bf16[128,512]{1,0:T(8,128)(2,1)S(1)}, bf16[128,512]{1,0:T(8,128)(2,1)S(1)}, u32[]{:S(2)}, u32[]{:S(2)}) %collective-permute-start.4) | collective-permute-done | bytes 131104 | tf_op jit(solution)/shard_map/ppermute | solution.py:316
  28.9 2.9 %collective-permute-done.3.refs_1_ = bf16[128,512]{1,0:T(8,128)(2,1)S(1)} collective-permute-done((bf16[128,512]{1,0:T(8,128)(2,1)S(1)}, bf16[128,512]{1,0:T(8,128)(2,1)S(1)}, u32[]{:S(2)}, u32[]{:S(2)}) %collective-permute-start.3) | collective-permute-done | bytes 131104 | tf_op jit(solution)/shard_map/ppermute | solution.py:316
  31.8 1.9 %collective-permute-start.9 = (bf16[2,512,512]{2,1,0:T(8,128)(2,1)}, bf16[2,512,512]{2,1,0:T(8,128)(2,1)}, u32[]{:S(2)}, u32[]{:S(2)}) collective-permute-start(bf16[2,512,512]{2,1,0:T(8,128)(2,1)} %get-tuple-element.34), channel_id=1, source_target_pairs={{0,4},{4,8},{8,12},{1,5},{5,9},{9,13},{2,6},{6,10},{10,14},{3,7},{... | collective-permute-start | bytes 3145736 | tf_op jit(solution)/shard_map/ppermute | solution.py:339
  33.8 3.9 %collective-permute-start.10 = (bf16[2,512,512]{2,1,0:T(8,128)(2,1)}, bf16[2,512,512]{2,1,0:T(8,128)(2,1)}, u32[]{:S(2)}, u32[]{:S(2)}) collective-permute-start(bf16[2,512,512]{2,1,0:T(8,128)(2,1)} %get-tuple-element.35), channel_id=1, source_target_pairs={{4,0},{8,4},{12,8},{5,1},{9,5},{13,9},{6,2},{10,6},{14,10},{7,3},{... | collective-permute-start | bytes 3145736 | tf_op jit(solution)/shard_map/ppermute | solution.py:340
  37.7 1.1 fusion.12.limits_ref
  38.8 9.6 %pack_attention.1 = bf16[512,640]{1,0:T(8,128)(2,1)S(1)} custom-call(bf16[2,1024,512]{2,1,0:T(8,128)(2,1)S(1)} %copy-done.2, bf16[128,512]{1,0:T(8,128)(2,1)S(1)} %fusion.4.refs_0_, bf16[128,512]{1,0:T(8,128)(2,1)S(1)} %collective-permute-done.3.refs_1_, bf16[128,512]{1,0:T(8,128)(2,1)S(1)} %collective-permute-done.4.refs_2_, ...), custom_call_target="tpu_custom_call" | custom-call | flops 4294967296 | bytes 4194304 | tf_op jit(solution)/shard_map/pack_attention/pallas_call | solution.py:93
  48.4 0.7 fusion.9
  49.2 0.5 collective-permute-start.8
  49.7 2.8 %collective-permute-start.7 = (bf16[128,640]{1,0:T(8,128)(2,1)S(1)}, bf16[128,640]{1,0:T(8,128)(2,1)S(1)}, u32[]{:S(2)}, u32[]{:S(2)}) collective-permute-start(bf16[128,640]{1,0:T(8,128)(2,1)S(1)} %get-tuple-element.56), channel_id=1, source_target_pairs={{0,8},{4,12},{8,0},{12,4},{1,9},{5,13},{9,1},{13,5},{2,10},{6,14},... | collective-permute-start | bytes 491528 | tf_op jit(solution)/shard_map/ppermute | solution.py:316
  52.8 19.1 %collective-permute-done.8.refs_3_ = bf16[128,640]{1,0:T(8,128)(2,1)S(1)} collective-permute-done((bf16[128,640]{1,0:T(8,128)(2,1)S(1)}, bf16[128,640]{1,0:T(8,128)(2,1)S(1)}, u32[]{:S(2)}, u32[]{:S(2)}) %collective-permute-start.8) | collective-permute-done | bytes 163872 | tf_op jit(solution)/shard_map/ppermute | solution.py:316
  71.8 1.8 %collective-permute-done.7.refs_2_ = bf16[128,640]{1,0:T(8,128)(2,1)S(1)} collective-permute-done((bf16[128,640]{1,0:T(8,128)(2,1)S(1)}, bf16[128,640]{1,0:T(8,128)(2,1)S(1)}, u32[]{:S(2)}, u32[]{:S(2)}) %collective-permute-start.7) | collective-permute-done | bytes 163872 | tf_op jit(solution)/shard_map/ppermute | solution.py:316
  73.6 0.7 copy-done.8
  74.3 2.7 %combine.1 = bf16[128,512]{1,0:T(8,128)(2,1)} custom-call(bf16[128,640]{1,0:T(8,128)(2,1)} %get-tuple-element.58.refs_0_, bf16[128,640]{1,0:T(8,128)(2,1)} %copy-done.9, bf16[128,640]{1,0:T(8,128)(2,1)} %copy-done.8, bf16[128,640]{1,0:T(8,128)(2,1)} %copy-done.7), custom_call_target="tpu_custom_call" | custom-call | tf_op jit(solution)/shard_map/combine/pallas_call | solution.py:135
  77.0 0.5 collective-permute-start.12
  77.8 11.9 %window_attention.2 = (f32[1024,512]{1,0:T(8,128)S(1)}, f32[1024,512]{1,0:T(8,128)}) custom-call(s32[8]{0:T(128)S(1)} %copy-done.4, s32[2048]{0:T(1024)S(1)} %bitcast.17, bf16[1024,512]{1,0:T(8,128)(2,1)S(1)} %copy-done.3, bf16[2,1024,512]{2,1,0:T(8,128)(2,1)} %own_ref.3, bf16[2,512,512]{2,1,0:T(8,128)(2,1)} %collective-permute-done.9.left_ref, ...), custom_call_target="tpu_custom_call" | custom-call | flops 2684354560 | bytes 2621440 | tf_op jit(solution)/shard_map/window_attention/pallas_call | solution.py:201
  89.8 2.2 %project.1.refs_0_ = bf16[2,128,512]{2,1,0:T(8,128)(2,1)S(1)} custom-call(s32[4]{0:T(128)S(1)} %and_select_fusion.1.order_ref, bf16[4,128,512]{2,1,0:T(8,128)(2,1)S(1)} %pad_maximum_fusion.part_ref, bf16[2,2048,512]{2,1,0:T(8,128)(2,1)S(1)} %copy-done.1), custom_call_target="tpu_custom_call" | custom-call | tf_op jit(solution)/shard_map/project/pallas_call | solution.py:297
  92.1 2.1 %collective-permute-start.15 = (bf16[2,128,512]{2,1,0:T(8,128)(2,1)S(1)}, bf16[2,128,512]{2,1,0:T(8,128)(2,1)S(1)}, u32[]{:S(2)}, u32[]{:S(2)}) collective-permute-start(bf16[2,128,512]{2,1,0:T(8,128)(2,1)S(1)} %project.1.refs_0_), channel_id=1, source_target_pairs={{0,8},{4,12},{8,0},{12,4},{1,9},{5,13},{9,1},{13,5},{2,10},{6,14},... | collective-permute-start | bytes 786440 | tf_op jit(solution)/shard_map/ppermute | solution.py:316
  94.2 1.9 %collective-permute-start.14 = (bf16[2,128,512]{2,1,0:T(8,128)(2,1)S(1)}, bf16[2,128,512]{2,1,0:T(8,128)(2,1)S(1)}, u32[]{:S(2)}, u32[]{:S(2)}) collective-permute-start(bf16[2,128,512]{2,1,0:T(8,128)(2,1)S(1)} %project.1.refs_0_), channel_id=1, source_target_pairs={{0,4},{4,8},{8,12},{12,0},{1,5},{5,9},{9,13},{13,1},{2,6},{6,10},{... | collective-permute-start | bytes 786440 | tf_op jit(solution)/shard_map/ppermute | solution.py:316
  96.2 27.8 %window_attention.3 = (f32[1024,512]{1,0:T(8,128)S(1)}, f32[1024,512]{1,0:T(8,128)}) custom-call(s32[8]{0:T(128)S(1)} %copy-done.4, s32[2048]{0:T(1024)S(1)} %bitcast.18, bf16[1024,512]{1,0:T(8,128)(2,1)S(1)} %copy-done.3, bf16[2,1024,512]{2,1,0:T(8,128)(2,1)} %own_ref.3, ...), custom_call_target="tpu_custom_call", output_to_operand_aliasing={{0}: (7, {}), {1}: (8, {})} | custom-call | flops 8053063680 | bytes 7864320 | tf_op jit(solution)/shard_map/window_attention/pallas_call | solution.py:201
  124.0 13.3 %final_attention.1 = bf16[1024,512]{1,0:T(8,128)(2,1)} custom-call(bf16[1024,512]{1,0:T(8,128)(2,1)S(1)} %copy-done.3, f32[1024,512]{1,0:T(8,128)S(1)} %get-tuple-element.47.part_ref, f32[1024,512]{1,0:T(8,128)} %get-tuple-element.48.lse_ref, bf16[2,128,512]{2,1,0:T(8,128)(2,1)S(1)} %project.1.refs_0_, ...), custom_call_target="tpu_custom_call" | custom-call | flops 4294967296 | bytes 6291456 | tf_op jit(solution)/shard_map/final_attention/pallas_call | solution.py:261
  (46 shorter events, 1.3 us)
Async XLA Ops:
  0.0 0.7 copy-start
  1.3 20.2 %copy-start.2 = (bf16[2,1024,512]{2,1,0:T(8,128)(2,1)S(1)}, bf16[2,1024,512]{2,1,0:T(8,128)(2,1)}, u32[]{:S(2)}) copy-start(bf16[2,1024,512]{2,1,0:T(8,128)(2,1)} %own_ref.3) | copy-start | bytes 6291460
  3.4 11.4 %collective-permute-start = (bf16[128,512]{1,0:T(8,128)(2,1)S(1)}, bf16[128,512]{1,0:T(8,128)(2,1)S(1)}, u32[]{:S(2)}, u32[]{:S(2)}) collective-permute-start(bf16[128,512]{1,0:T(8,128)(2,1)S(1)} %get-tuple-element.59), channel_id=1, source_target_pairs={{0,4},{4,8},{8,12},{12,0},{1,5},{5,9},{9,13},{13,1},{2,6},{6,10},{... | collective-permute-start | bytes 393224 | tf_op jit(solution)/shard_map/ppermute | solution.py:316
  5.1 9.8 %collective-permute-start.2 = (bf16[128,512]{1,0:T(8,128)(2,1)S(1)}, bf16[128,512]{1,0:T(8,128)(2,1)S(1)}, u32[]{:S(2)}, u32[]{:S(2)}) collective-permute-start(bf16[128,512]{1,0:T(8,128)(2,1)S(1)} %get-tuple-element.60), channel_id=1, source_target_pairs={{0,12},{4,0},{8,4},{12,8},{1,13},{5,1},{9,5},{13,9},{2,14},{6,2},{... | collective-permute-start | bytes 393224 | tf_op jit(solution)/shard_map/ppermute | solution.py:316
  5.5 10.5 %collective-permute-start.1 = (bf16[128,512]{1,0:T(8,128)(2,1)S(1)}, bf16[128,512]{1,0:T(8,128)(2,1)S(1)}, u32[]{:S(2)}, u32[]{:S(2)}) collective-permute-start(bf16[128,512]{1,0:T(8,128)(2,1)S(1)} %get-tuple-element.61), channel_id=1, source_target_pairs={{0,8},{4,12},{8,0},{12,4},{1,9},{5,13},{9,1},{13,5},{2,10},{6,14},... | collective-permute-start | bytes 393224 | tf_op jit(solution)/shard_map/ppermute | solution.py:316
  16.0 6.9 %copy-start.10 = (s32[2,1024]{1,0:T(2,128)S(1)}, s32[2,1024]{1,0:T(2,128)}, u32[]{:S(2)}) copy-start(s32[2,1024]{1,0:T(2,128)} %param.9) | copy-start | bytes 24580
  16.0 8.0 %collective-permute-start.5 = (bf16[128,512]{1,0:T(8,128)(2,1)S(1)}, bf16[128,512]{1,0:T(8,128)(2,1)S(1)}, u32[]{:S(2)}, u32[]{:S(2)}) collective-permute-start(bf16[128,512]{1,0:T(8,128)(2,1)S(1)} %fusion.4.refs_0_), channel_id=1, source_target_pairs={{0,12},{4,0},{8,4},{12,8},{1,13},{5,1},{9,5},{13,9},{2,14},{6,2},{... | collective-permute-start | bytes 393224 | tf_op jit(solution)/shard_map/ppermute | solution.py:316
  16.8 12.1 %collective-permute-start.4 = (bf16[128,512]{1,0:T(8,128)(2,1)S(1)}, bf16[128,512]{1,0:T(8,128)(2,1)S(1)}, u32[]{:S(2)}, u32[]{:S(2)}) collective-permute-start(bf16[128,512]{1,0:T(8,128)(2,1)S(1)} %fusion.4.refs_0_), channel_id=1, source_target_pairs={{0,8},{4,12},{8,0},{12,4},{1,9},{5,13},{9,1},{13,5},{2,10},{6,14},... | collective-permute-start | bytes 393224 | tf_op jit(solution)/shard_map/ppermute | solution.py:316
  21.1 10.8 %collective-permute-start.3 = (bf16[128,512]{1,0:T(8,128)(2,1)S(1)}, bf16[128,512]{1,0:T(8,128)(2,1)S(1)}, u32[]{:S(2)}, u32[]{:S(2)}) collective-permute-start(bf16[128,512]{1,0:T(8,128)(2,1)S(1)} %fusion.4.refs_0_), channel_id=1, source_target_pairs={{0,4},{4,8},{8,12},{12,0},{1,5},{5,9},{9,13},{13,1},{2,6},{6,10},{... | collective-permute-start | bytes 393224 | tf_op jit(solution)/shard_map/ppermute | solution.py:316
  31.8 45.9 %collective-permute-start.9 = (bf16[2,512,512]{2,1,0:T(8,128)(2,1)}, bf16[2,512,512]{2,1,0:T(8,128)(2,1)}, u32[]{:S(2)}, u32[]{:S(2)}) collective-permute-start(bf16[2,512,512]{2,1,0:T(8,128)(2,1)} %get-tuple-element.34), channel_id=1, source_target_pairs={{0,4},{4,8},{8,12},{1,5},{5,9},{9,13},{2,6},{6,10},{10,14},{3,7},{... | collective-permute-start | bytes 3145736 | tf_op jit(solution)/shard_map/ppermute | solution.py:339
  33.8 44.0 %collective-permute-start.10 = (bf16[2,512,512]{2,1,0:T(8,128)(2,1)}, bf16[2,512,512]{2,1,0:T(8,128)(2,1)}, u32[]{:S(2)}, u32[]{:S(2)}) collective-permute-start(bf16[2,512,512]{2,1,0:T(8,128)(2,1)} %get-tuple-element.35), channel_id=1, source_target_pairs={{4,0},{8,4},{12,8},{5,1},{9,5},{13,9},{6,2},{10,6},{14,10},{7,3},{... | collective-permute-start | bytes 3145736 | tf_op jit(solution)/shard_map/ppermute | solution.py:340
  38.8 13.7 %copy-start.5 = (s32[2,1024]{0,1:T(8,128)S(1)}, s32[2,1024]{0,1:T(8,128)}, u32[]{:S(2)}) copy-start(s32[2,1024]{0,1:T(8,128)} %copy.12) | copy-start | bytes 24580
  48.4 29.4 %copy-start.3 = (bf16[1024,512]{1,0:T(8,128)(2,1)S(1)}, bf16[1024,512]{1,0:T(8,128)(2,1)}, u32[]{:S(2)}) copy-start(bf16[1024,512]{1,0:T(8,128)(2,1)} %q_ref.5) | copy-start | bytes 3145732
  48.4 29.4 %copy-start.4 = (s32[8]{0:T(128)S(1)}, s32[8]{0:T(128)}, u32[]{:S(2)}) copy-start(s32[8]{0:T(128)} %radius_ref.1) | copy-start | bytes 100
  49.2 22.7 %collective-permute-start.8 = (bf16[128,640]{1,0:T(8,128)(2,1)S(1)}, bf16[128,640]{1,0:T(8,128)(2,1)S(1)}, u32[]{:S(2)}, u32[]{:S(2)}) collective-permute-start(bf16[128,640]{1,0:T(8,128)(2,1)S(1)} %get-tuple-element.55), channel_id=1, source_target_pairs={{0,12},{4,0},{8,4},{12,8},{1,13},{5,1},{9,5},{13,9},{2,14},{6,2},{... | collective-permute-start | bytes 491528 | tf_op jit(solution)/shard_map/ppermute | solution.py:316
  49.7 23.9 %collective-permute-start.7 = (bf16[128,640]{1,0:T(8,128)(2,1)S(1)}, bf16[128,640]{1,0:T(8,128)(2,1)S(1)}, u32[]{:S(2)}, u32[]{:S(2)}) collective-permute-start(bf16[128,640]{1,0:T(8,128)(2,1)S(1)} %get-tuple-element.56), channel_id=1, source_target_pairs={{0,8},{4,12},{8,0},{12,4},{1,9},{5,13},{9,1},{13,5},{2,10},{6,14},... | collective-permute-start | bytes 491528 | tf_op jit(solution)/shard_map/ppermute | solution.py:316
  52.5 21.1 %collective-permute-start.6 = (bf16[128,640]{1,0:T(8,128)(2,1)S(1)}, bf16[128,640]{1,0:T(8,128)(2,1)S(1)}, u32[]{:S(2)}, u32[]{:S(2)}) collective-permute-start(bf16[128,640]{1,0:T(8,128)(2,1)S(1)} %get-tuple-element.57), channel_id=1, source_target_pairs={{0,4},{4,8},{8,12},{12,0},{1,5},{5,9},{9,13},{13,1},{2,6},{6,10},{... | collective-permute-start | bytes 491528 | tf_op jit(solution)/shard_map/ppermute | solution.py:316
  71.8 1.8 %copy-start.7 = (bf16[128,640]{1,0:T(8,128)(2,1)}, bf16[128,640]{1,0:T(8,128)(2,1)S(1)}, u32[]{:S(2)}) copy-start(bf16[128,640]{1,0:T(8,128)(2,1)S(1)} %collective-permute-done.8.refs_3_) | copy-start | bytes 491524
  73.6 0.7 copy-start.8
  73.6 0.7 copy-start.9
  77.0 12.7 %collective-permute-start.13 = (bf16[128,512]{1,0:T(8,128)(2,1)}, bf16[128,512]{1,0:T(8,128)(2,1)S(1)}, u32[]{:S(2)}, u32[]{:S(2)}) collective-permute-start(bf16[128,512]{1,0:T(8,128)(2,1)} %combine.1), channel_id=1, source_target_pairs={{0,3},{1,0},{2,1},{3,2},{4,7},{5,4},{6,5},{7,6},{8,11},{9,8},{10,9... | collective-permute-start | bytes 393224 | tf_op jit(solution)/shard_map/ppermute | solution.py:316
  77.0 12.7 %collective-permute-start.12 = (bf16[128,512]{1,0:T(8,128)(2,1)}, bf16[128,512]{1,0:T(8,128)(2,1)S(1)}, u32[]{:S(2)}, u32[]{:S(2)}) collective-permute-start(bf16[128,512]{1,0:T(8,128)(2,1)} %combine.1), channel_id=1, source_target_pairs={{0,2},{1,3},{2,0},{3,1},{4,6},{5,7},{6,4},{7,5},{8,10},{9,11},{10,... | collective-permute-start | bytes 393224 | tf_op jit(solution)/shard_map/ppermute | solution.py:316
  77.5 12.2 %collective-permute-start.11 = (bf16[128,512]{1,0:T(8,128)(2,1)}, bf16[128,512]{1,0:T(8,128)(2,1)S(1)}, u32[]{:S(2)}, u32[]{:S(2)}) collective-permute-start(bf16[128,512]{1,0:T(8,128)(2,1)} %combine.1), channel_id=1, source_target_pairs={{0,1},{1,2},{2,3},{3,0},{4,5},{5,6},{6,7},{7,4},{8,9},{9,10},{10,1... | collective-permute-start | bytes 393224 | tf_op jit(solution)/shard_map/ppermute | solution.py:316
  77.8 11.9 %copy-start.6 = (bf16[128,512]{1,0:T(8,128)(2,1)S(1)}, bf16[128,512]{1,0:T(8,128)(2,1)}, u32[]{:S(2)}) copy-start(bf16[128,512]{1,0:T(8,128)(2,1)} %combine.1) | copy-start | bytes 393220
  77.8 12.0 %copy-start.1 = (bf16[2,2048,512]{2,1,0:T(8,128)(2,1)S(1)}, bf16[2,2048,512]{2,1,0:T(8,128)(2,1)}, u32[]{:S(2)}) copy-start(bf16[2,2048,512]{2,1,0:T(8,128)(2,1)} %proj_ref.1) | copy-start | bytes 12582916
  92.0 32.0 %collective-permute-start.16 = (bf16[2,128,512]{2,1,0:T(8,128)(2,1)S(1)}, bf16[2,128,512]{2,1,0:T(8,128)(2,1)S(1)}, u32[]{:S(2)}, u32[]{:S(2)}) collective-permute-start(bf16[2,128,512]{2,1,0:T(8,128)(2,1)S(1)} %project.1.refs_0_), channel_id=1, source_target_pairs={{0,12},{4,0},{8,4},{12,8},{1,13},{5,1},{9,5},{13,9},{2,14},{6,2},{... | collective-permute-start | bytes 786440 | tf_op jit(solution)/shard_map/ppermute | solution.py:316
  92.1 31.9 %collective-permute-start.15 = (bf16[2,128,512]{2,1,0:T(8,128)(2,1)S(1)}, bf16[2,128,512]{2,1,0:T(8,128)(2,1)S(1)}, u32[]{:S(2)}, u32[]{:S(2)}) collective-permute-start(bf16[2,128,512]{2,1,0:T(8,128)(2,1)S(1)} %project.1.refs_0_), channel_id=1, source_target_pairs={{0,8},{4,12},{8,0},{12,4},{1,9},{5,13},{9,1},{13,5},{2,10},{6,14},... | collective-permute-start | bytes 786440 | tf_op jit(solution)/shard_map/ppermute | solution.py:316
  94.2 29.8 %collective-permute-start.14 = (bf16[2,128,512]{2,1,0:T(8,128)(2,1)S(1)}, bf16[2,128,512]{2,1,0:T(8,128)(2,1)S(1)}, u32[]{:S(2)}, u32[]{:S(2)}) collective-permute-start(bf16[2,128,512]{2,1,0:T(8,128)(2,1)S(1)} %project.1.refs_0_), channel_id=1, source_target_pairs={{0,4},{4,8},{8,12},{12,0},{1,5},{5,9},{9,13},{13,1},{2,6},{6,10},{... | collective-permute-start | bytes 786440 | tf_op jit(solution)/shard_map/ppermute | solution.py:316
where the time goes:
time: 138 us; the launch traced here: 137 us
  Pallas kernels  67.5 us (49%)
  waiting for transfers between devices  37 us (27%)
  starting transfers between devices  23.8 us (17%)
  local copies, waits for them, and re-layouts  5.45 us (4%)
  matrix products  2.13 us (2%)
    pallas_call x2, Pallas kernels, window_attention(): pl.pallas_call(functools.partial(window_kernel, pairs[0]), grid_spec=pltp...  39.7 us
    ppermute x15, waiting for transfers between devices, shifted(): lax.ppermute(x, axis, [(i, (i + shift) % count) for i in range(count)])  37 us
    ppermute x15, starting transfers between devices, shifted(): lax.ppermute(x, axis, [(i, (i + shift) % count) for i in range(count)])  18 us
    pallas_call x1, Pallas kernels, final_attention(): pl.pallas_call(final_kernel, grid=(width // PAIR,), in_specs=[spec] * 3 +...  13.3 us
    pallas_call x1, Pallas kernels, pack_attention(): pl.pallas_call(pack_kernel, grid=(width // PAIR,), in_specs=[pl.BlockSpec...  9.6 us
    ppermute x1, starting transfers between devices, shards(): right = lax.ppermute(head, 'seq', [(i + 1, i) for i in range(ends)])  3.92 us
  transfers between devices with their start and end apart: 17, of which 6 were waited for; matrix products, arithmetic and copies ran while one was open for 3% of the time, Pallas kernels for 38%

commit v1 on v0

--- a/solution.py
+++ b/solution.py
@@ -206,8 +206,8 @@
             in_specs=[
                 spec((tokens, PAIR)),
                 spec((2, tokens, PAIR)),
-                spec((2, RADIUS, PAIR)),
-                spec((2, RADIUS, PAIR)),
+                pl.BlockSpec((2, RADIUS, PAIR), lambda i, *_: (0, 0, i)),
+                pl.BlockSpec((2, RADIUS, PAIR), lambda i, *_: (0, 0, i)),
                 pl.BlockSpec((tokens, 2), lambda i, *_: (0, 0)),
             ]
             + [pl.BlockSpec(memory_space=pl.ANY)] * len(done),
@@ -333,41 +333,48 @@
         mine = mine + shifted(picked[s], "seq", count, s)
     pack_query = [mine] + [shifted(mine, "seq", count, s) for s in range(1, count)]
 
-    ends = count - 1
-    tail, head = keys_values[:, tokens - RADIUS :], keys_values[:, :RADIUS]
-    pack_query, tail, head = lax.optimization_barrier((pack_query, tail, head))
-    left = lax.ppermute(tail, "seq", [(i, i + 1) for i in range(ends)])
-    right = lax.ppermute(head, "seq", [(i + 1, i) for i in range(ends)])
-
     limits = bounds - (first_pos - RADIUS)
     pairs = width // PAIR
     edges = [0, 0, pairs // 4, pairs]
     window = ()
 
-    def windowed(stage, after, beside):
+    def halos(stage, after):
+        columns = slice(edges[stage] * PAIR, edges[stage + 1] * PAIR)
+        tail, head = keys_values[:, tokens - RADIUS :, columns], keys_values[:, :RADIUS, columns]
+        if tail.shape[2] == 0:
+            return (), after
+        after, tail, head = lax.optimization_barrier((after, tail, head))
+        ends = count - 1
+        left = lax.ppermute(tail, "seq", [(i, i + 1) for i in range(ends)])
+        right = lax.ppermute(head, "seq", [(i + 1, i) for i in range(ends)])
+        return (left, right), after
+
+    def windowed(stage, after, beside, sides):
         nonlocal window
         if edges[stage] == edges[stage + 1]:
             return beside
         held, _ = lax.optimization_barrier((radius, after))
         window = window_attention(
-            queries, keys_values, left, right, limits, held, edges[stage : stage + 2], window
+            queries, keys_values, *sides, limits, held, edges[stage : stage + 2], window
         )
         *window, beside = lax.optimization_barrier((*window, beside))
         return beside
 
+    early, pack_query = halos(1, pack_query)
     part = pack_attention(pack_query, keys_values).reshape(count, share, width + 128)
     parts = [part[0]] + [shifted(part[count - s], "seq", count, s) for s in range(1, count)]
-    packed = combine(windowed(0, part, parts))
+    early, parts = lax.optimization_barrier((early, parts))
+    late, packed = halos(2, combine(parts))
 
     axes = ("head", "rep")
     sides = lax.axis_size("head") * lax.axis_size("rep")
     here = lax.axis_index("head") * lax.axis_size("rep") + lax.axis_index("rep")
     gathered = [packed] + [shifted(packed, axes, sides, s) for s in range(1, sides)]
-    gathered = jnp.stack(windowed(1, packed, gathered))
+    gathered = jnp.stack(windowed(1, packed, gathered, early))
     order = (here - jnp.arange(sides, dtype=jnp.int32)) % sides
     pack_share = project(order, gathered, pack_proj)
     shares = [pack_share] + [shifted(pack_share, "seq", count, s) for s in range(1, count)]
-    shares = windowed(2, pack_share, shares)
+    shares = windowed(2, pack_share, shares, late)
     return final_attention(queries, shares, *window)
 
 

time: 138 us -> 138 us (level)
  the two profiles are of different devices: /device:TPU:18 before, /device:TPU:9 now
where the time goes in v1:
time: 138 us; the launch traced here: 137 us
  Pallas kernels  65.6 us (48%)
  starting transfers between devices  31.6 us (23%)
  waiting for transfers between devices  28.2 us (20%)
  local copies, waits for them, and re-layouts  6.31 us (5%)
  other arithmetic  3.09 us (2%)
  matrix products  2.13 us (2%)
    pallas_call x2, Pallas kernels, window_attention(): pl.pallas_call(functools.partial(window_kernel, pairs[0]), grid_spec=pltp...  37.8 us
    ppermute x15, waiting for transfers between devices, shifted(): lax.ppermute(x, axis, [(i, (i + shift) % count) for i in range(count)])  28.2 us
    ppermute x15, starting transfers between devices, shifted(): lax.ppermute(x, axis, [(i, (i + shift) % count) for i in range(count)])  19.5 us
    pallas_call x1, Pallas kernels, final_attention(): pl.pallas_call(final_kernel, grid=(width // PAIR,), in_specs=[spec] * 3 +...  13.3 us
    pallas_call x1, Pallas kernels, pack_attention(): pl.pallas_call(pack_kernel, grid=(width // PAIR,), in_specs=[pl.BlockSpec...  9.6 us
    ppermute x2, starting transfers between devices, halos(): left = lax.ppermute(tail, 'seq', [(i, i + 1) for i in range(ends)])  8.32 us
    ppermute x2, starting transfers between devices, halos(): right = lax.ppermute(head, 'seq', [(i + 1, i) for i in range(ends)])  3.84 us
  transfers between devices with their start and end apart: 19, of which 7 were waited for; matrix products, arithmetic and copies ran while one was open for 5% of the time, Pallas kernels for 36%

profile of v1, /device:TPU:9, one launch (start us, length us, event | category | flops | bytes accessed | tf_op | source)
XLA Modules:
  0.0 137.1 jit_solution(16140710568270775589)
XLA Ops:
  1.3 2.1 %fusion.1 = bf16[512,512]{1,0:T(8,128)(2,1)S(1)} fusion(bf16[1024,512]{1,0:T(8,128)(2,1)} %q_ref.5, s32[512]{0:T(512)S(1)} %subtract_bitcast_fusion), kind=kOutput, calls=%fused_computation.3 | convolution fusion | flops 537657344 | bytes 1574912 | tf_op jit(solution)/shard_map/dot_general | solution.py:329
  3.4 1.3 collective-permute-start
  5.0 2.3 %collective-permute-start.1 = (bf16[128,512]{1,0:T(8,128)(2,1)S(1)}, bf16[128,512]{1,0:T(8,128)(2,1)S(1)}, u32[]{:S(2)}, u32[]{:S(2)}) collective-permute-start(bf16[128,512]{1,0:T(8,128)(2,1)S(1)} %get-tuple-element.81), channel_id=1, source_target_pairs={{0,8},{4,12},{8,0},{12,4},{1,9},{5,13},{9,1},{13,5},{2,10},{6,14},... | collective-permute-start | bytes 393224 | tf_op jit(solution)/shard_map/ppermute | solution.py:316
  7.3 1.0 copy.12
  8.3 5.0 %collective-permute-done.2 = bf16[128,512]{1,0:T(8,128)(2,1)S(1)} collective-permute-done((bf16[128,512]{1,0:T(8,128)(2,1)S(1)}, bf16[128,512]{1,0:T(8,128)(2,1)S(1)}, u32[]{:S(2)}, u32[]{:S(2)}) %collective-permute-start.2) | collective-permute-done | bytes 131104 | tf_op jit(solution)/shard_map/ppermute | solution.py:316
  13.3 2.7 %collective-permute-done.1 = bf16[128,512]{1,0:T(8,128)(2,1)S(1)} collective-permute-done((bf16[128,512]{1,0:T(8,128)(2,1)S(1)}, bf16[128,512]{1,0:T(8,128)(2,1)S(1)}, u32[]{:S(2)}, u32[]{:S(2)}) %collective-permute-start.1) | collective-permute-done | bytes 131104 | tf_op jit(solution)/shard_map/ppermute | solution.py:316
  16.0 3.4 %collective-permute-start.5 = (bf16[128,512]{1,0:T(8,128)(2,1)S(1)}, bf16[128,512]{1,0:T(8,128)(2,1)S(1)}, u32[]{:S(2)}, u32[]{:S(2)}) collective-permute-start(bf16[128,512]{1,0:T(8,128)(2,1)S(1)} %fusion.4.refs_0_), channel_id=1, source_target_pairs={{0,12},{4,0},{8,4},{12,8},{1,13},{5,1},{9,5},{13,9},{2,14},{6,2},{... | collective-permute-start | bytes 393224 | tf_op jit(solution)/shard_map/ppermute | solution.py:316
  19.5 2.1 %collective-permute-start.3 = (bf16[128,512]{1,0:T(8,128)(2,1)S(1)}, bf16[128,512]{1,0:T(8,128)(2,1)S(1)}, u32[]{:S(2)}, u32[]{:S(2)}) collective-permute-start(bf16[128,512]{1,0:T(8,128)(2,1)S(1)} %fusion.4.refs_0_), channel_id=1, source_target_pairs={{0,4},{4,8},{8,12},{12,0},{1,5},{5,9},{9,13},{13,1},{2,6},{6,10},{... | collective-permute-start | bytes 393224 | tf_op jit(solution)/shard_map/ppermute | solution.py:316
  21.8 5.3 %collective-permute-done.4.refs_2_ = bf16[128,512]{1,0:T(8,128)(2,1)S(1)} collective-permute-done((bf16[128,512]{1,0:T(8,128)(2,1)S(1)}, bf16[128,512]{1,0:T(8,128)(2,1)S(1)}, u32[]{:S(2)}, u32[]{:S(2)}) %collective-permute-start.4) | collective-permute-done | bytes 131104 | tf_op jit(solution)/shard_map/ppermute | solution.py:316
  27.1 3.3 %collective-permute-done.3.refs_1_ = bf16[128,512]{1,0:T(8,128)(2,1)S(1)} collective-permute-done((bf16[128,512]{1,0:T(8,128)(2,1)S(1)}, bf16[128,512]{1,0:T(8,128)(2,1)S(1)}, u32[]{:S(2)}, u32[]{:S(2)}) %collective-permute-start.3) | collective-permute-done | bytes 131104 | tf_op jit(solution)/shard_map/ppermute | solution.py:316
  30.5 4.1 %collective-permute-start.6 = (bf16[2,512,128]{2,1,0:T(8,128)(2,1)S(1)}, bf16[2,512,128]{2,1,0:T(8,128)(2,1)S(1)}, u32[]{:S(2)}, u32[]{:S(2)}) collective-permute-start(bf16[2,512,128]{2,1,0:T(8,128)(2,1)S(1)} %get-tuple-element.38), channel_id=1, source_target_pairs={{0,4},{4,8},{8,12},{1,5},{5,9},{9,13},{2,6},{6,10},{10,14},{3,7},{... | collective-permute-start | bytes 786440 | tf_op jit(solution)/shard_map/ppermute | solution.py:348
  34.6 1.9 %collective-permute-start.7 = (bf16[2,512,128]{2,1,0:T(8,128)(2,1)S(1)}, bf16[2,512,128]{2,1,0:T(8,128)(2,1)S(1)}, u32[]{:S(2)}, u32[]{:S(2)}) collective-permute-start(bf16[2,512,128]{2,1,0:T(8,128)(2,1)S(1)} %get-tuple-element.39), channel_id=1, source_target_pairs={{4,0},{8,4},{12,8},{5,1},{9,5},{13,9},{6,2},{10,6},{14,10},{7,3},{... | collective-permute-start | bytes 786440 | tf_op jit(solution)/shard_map/ppermute | solution.py:349
  36.5 9.6 %pack_attention.1 = bf16[512,640]{1,0:T(8,128)(2,1)S(1)} custom-call(bf16[2,1024,512]{2,1,0:T(8,128)(2,1)S(1)} %copy-done.2, bf16[128,512]{1,0:T(8,128)(2,1)S(1)} %fusion.4.refs_0_, bf16[128,512]{1,0:T(8,128)(2,1)S(1)} %collective-permute-done.3.refs_1_, bf16[128,512]{1,0:T(8,128)(2,1)S(1)} %collective-permute-done.4.refs_2_, ...), custom_call_target="tpu_custom_call" | custom-call | flops 4294967296 | bytes 4194304 | tf_op jit(solution)/shard_map/pack_attention/pallas_call | solution.py:93
  46.8 2.6 %collective-permute-start.9 = (bf16[128,640]{1,0:T(8,128)(2,1)S(1)}, bf16[128,640]{1,0:T(8,128)(2,1)S(1)}, u32[]{:S(2)}, u32[]{:S(2)}) collective-permute-start(bf16[128,640]{1,0:T(8,128)(2,1)S(1)} %get-tuple-element.76), channel_id=1, source_target_pairs={{0,8},{4,12},{8,0},{12,4},{1,9},{5,13},{9,1},{13,5},{2,10},{6,14},... | collective-permute-start | bytes 491528 | tf_op jit(solution)/shard_map/ppermute | solution.py:316
  49.5 0.9 collective-permute-start.8
  50.4 1.3 fusion.8
  51.7 8.2 %collective-permute-done.9.refs_2_ = bf16[128,640]{1,0:T(8,128)(2,1)S(1)} collective-permute-done((bf16[128,640]{1,0:T(8,128)(2,1)S(1)}, bf16[128,640]{1,0:T(8,128)(2,1)S(1)}, u32[]{:S(2)}, u32[]{:S(2)}) %collective-permute-start.9) | collective-permute-done | bytes 163872 | tf_op jit(solution)/shard_map/ppermute | solution.py:316
  59.9 3.5 %collective-permute-done.8.refs_1_ = bf16[128,640]{1,0:T(8,128)(2,1)S(1)} collective-permute-done((bf16[128,640]{1,0:T(8,128)(2,1)S(1)}, bf16[128,640]{1,0:T(8,128)(2,1)S(1)}, u32[]{:S(2)}, u32[]{:S(2)}) %collective-permute-start.8) | collective-permute-done | bytes 163872 | tf_op jit(solution)/shard_map/ppermute | solution.py:316
  64.0 2.6 %combine.1 = bf16[128,512]{1,0:T(8,128)(2,1)} custom-call(bf16[128,640]{1,0:T(8,128)(2,1)} %get-tuple-element.44.refs_0_, bf16[128,640]{1,0:T(8,128)(2,1)} %copy-done.8, bf16[128,640]{1,0:T(8,128)(2,1)} %copy-done.7, bf16[128,640]{1,0:T(8,128)(2,1)} %copy-done.6), custom_call_target="tpu_custom_call" | custom-call | tf_op jit(solution)/shard_map/combine/pallas_call | solution.py:135
  66.7 4.2 %collective-permute-start.14 = (bf16[2,512,384]{2,1,0:T(8,128)(2,1)}, bf16[2,512,384]{2,1,0:T(8,128)(2,1)S(1)}, u32[]{:S(2)}, u32[]{:S(2)}) collective-permute-start(bf16[2,512,384]{2,1,0:T(8,128)(2,1)} %get-tuple-element.59), channel_id=1, source_target_pairs={{0,4},{4,8},{8,12},{1,5},{5,9},{9,13},{2,6},{6,10},{10,14},{3,7},{... | collective-permute-start | bytes 2359304 | tf_op jit(solution)/shard_map/ppermute | solution.py:348
  70.9 1.9 %collective-permute-start.15 = (bf16[2,512,384]{2,1,0:T(8,128)(2,1)}, bf16[2,512,384]{2,1,0:T(8,128)(2,1)S(1)}, u32[]{:S(2)}, u32[]{:S(2)}) collective-permute-start(bf16[2,512,384]{2,1,0:T(8,128)(2,1)} %get-tuple-element.60), channel_id=1, source_target_pairs={{4,0},{8,4},{12,8},{5,1},{9,5},{13,9},{6,2},{10,6},{14,10},{7,3},{... | collective-permute-start | bytes 2359304 | tf_op jit(solution)/shard_map/ppermute | solution.py:349
  72.9 1.9 %broadcast_subtract_fusion = s32[2,1024]{0,1:T(8,128)} fusion(s32[2,1024]{0,1:T(8,128)} %copy.12, s32[]{:T(128)S(6)} %sub.33), kind=kLoop, calls=%fused_computation.6 | loop fusion | flops 2048 | bytes 16388 | tf_op jit(solution)/shard_map/sub | solution.py:336
  74.7 1.2 copy.14
  76.0 1.1 fusion.13.limits_ref
  77.9 1.2 collective-permute-start.12
  79.1 1.2 collective-permute-start.11
  80.4 10.4 %window_attention.2 = (f32[1024,512]{1,0:T(8,128)S(1)}, f32[1024,512]{1,0:T(8,128)}) custom-call(s32[8]{0:T(128)S(1)} %copy-done.4, s32[2048]{0:T(1024)S(1)} %bitcast.17, bf16[1024,512]{1,0:T(8,128)(2,1)S(1)} %copy-done.3, bf16[2,1024,512]{2,1,0:T(8,128)(2,1)} %own_ref.3, bf16[2,512,128]{2,1,0:T(8,128)(2,1)S(1)} %collective-permute-done.6.left_ref, ...), custom_call_target="tpu_custom_call" | custom-call | flops 2684354560 | bytes 2621440 | tf_op jit(solution)/shard_map/window_attention/pallas_call | solution.py:201
  90.8 2.2 %project.1.refs_0_ = bf16[2,128,512]{2,1,0:T(8,128)(2,1)S(1)} custom-call(s32[4]{0:T(128)S(1)} %and_select_fusion.1.order_ref, bf16[4,128,512]{2,1,0:T(8,128)(2,1)S(1)} %pad_maximum_fusion.part_ref, bf16[2,2048,512]{2,1,0:T(8,128)(2,1)S(1)} %copy-done.1), custom_call_target="tpu_custom_call" | custom-call | tf_op jit(solution)/shard_map/project/pallas_call | solution.py:297
  93.1 2.1 %collective-permute-start.17 = (bf16[2,128,512]{2,1,0:T(8,128)(2,1)S(1)}, bf16[2,128,512]{2,1,0:T(8,128)(2,1)S(1)}, u32[]{:S(2)}, u32[]{:S(2)}) collective-permute-start(bf16[2,128,512]{2,1,0:T(8,128)(2,1)S(1)} %project.1.refs_0_), channel_id=1, source_target_pairs={{0,8},{4,12},{8,0},{12,4},{1,9},{5,13},{9,1},{13,5},{2,10},{6,14},... | collective-permute-start | bytes 786440 | tf_op jit(solution)/shard_map/ppermute | solution.py:316
  95.2 1.2 collective-permute-start.16
  96.4 27.5 %window_attention.3 = (f32[1024,512]{1,0:T(8,128)S(1)}, f32[1024,512]{1,0:T(8,128)}) custom-call(s32[8]{0:T(128)S(1)} %copy-done.4, s32[2048]{0:T(1024)S(1)} %bitcast.18, bf16[1024,512]{1,0:T(8,128)(2,1)S(1)} %copy-done.3, bf16[2,1024,512]{2,1,0:T(8,128)(2,1)} %own_ref.3, ...), custom_call_target="tpu_custom_call", output_to_operand_aliasing={{0}: (7, {}), {1}: (8, {})} | custom-call | flops 8053063680 | bytes 7864320 | tf_op jit(solution)/shard_map/window_attention/pallas_call | solution.py:201
  123.8 13.3 %final_attention.1 = bf16[1024,512]{1,0:T(8,128)(2,1)} custom-call(bf16[1024,512]{1,0:T(8,128)(2,1)S(1)} %copy-done.3, f32[1024,512]{1,0:T(8,128)S(1)} %get-tuple-element.65.part_ref, f32[1024,512]{1,0:T(8,128)} %get-tuple-element.66.lse_ref, bf16[2,128,512]{2,1,0:T(8,128)(2,1)S(1)} %project.1.refs_0_, ...), custom_call_target="tpu_custom_call" | custom-call | flops 4294967296 | bytes 6291456 | tf_op jit(solution)/shard_map/final_attention/pallas_call | solution.py:261
  (49 shorter events, 4.2 us)
Async XLA Ops:
  0.0 0.7 copy-start
  1.3 6.0 %copy-start.9 = (s32[2,1024]{1,0:T(2,128)S(1)}, s32[2,1024]{1,0:T(2,128)}, u32[]{:S(2)}) copy-start(s32[2,1024]{1,0:T(2,128)} %param.9) | copy-start | bytes 24580
  1.3 20.3 %copy-start.2 = (bf16[2,1024,512]{2,1,0:T(8,128)(2,1)S(1)}, bf16[2,1024,512]{2,1,0:T(8,128)(2,1)}, u32[]{:S(2)}) copy-start(bf16[2,1024,512]{2,1,0:T(8,128)(2,1)} %own_ref.3) | copy-start | bytes 6291460
  3.4 4.8 %collective-permute-start = (bf16[128,512]{1,0:T(8,128)(2,1)S(1)}, bf16[128,512]{1,0:T(8,128)(2,1)S(1)}, u32[]{:S(2)}, u32[]{:S(2)}) collective-permute-start(bf16[128,512]{1,0:T(8,128)(2,1)S(1)} %get-tuple-element.79), channel_id=1, source_target_pairs={{0,4},{4,8},{8,12},{12,0},{1,5},{5,9},{9,13},{13,1},{2,6},{6,10},{... | collective-permute-start | bytes 393224 | tf_op jit(solution)/shard_map/ppermute | solution.py:316
  4.8 8.5 %collective-permute-start.2 = (bf16[128,512]{1,0:T(8,128)(2,1)S(1)}, bf16[128,512]{1,0:T(8,128)(2,1)S(1)}, u32[]{:S(2)}, u32[]{:S(2)}) collective-permute-start(bf16[128,512]{1,0:T(8,128)(2,1)S(1)} %get-tuple-element.80), channel_id=1, source_target_pairs={{0,12},{4,0},{8,4},{12,8},{1,13},{5,1},{9,5},{13,9},{2,14},{6,2},{... | collective-permute-start | bytes 393224 | tf_op jit(solution)/shard_map/ppermute | solution.py:316
  5.0 11.0 %collective-permute-start.1 = (bf16[128,512]{1,0:T(8,128)(2,1)S(1)}, bf16[128,512]{1,0:T(8,128)(2,1)S(1)}, u32[]{:S(2)}, u32[]{:S(2)}) collective-permute-start(bf16[128,512]{1,0:T(8,128)(2,1)S(1)} %get-tuple-element.81), channel_id=1, source_target_pairs={{0,8},{4,12},{8,0},{12,4},{1,9},{5,13},{9,1},{13,5},{2,10},{6,14},... | collective-permute-start | bytes 393224 | tf_op jit(solution)/shard_map/ppermute | solution.py:316
  16.0 5.8 %collective-permute-start.5 = (bf16[128,512]{1,0:T(8,128)(2,1)S(1)}, bf16[128,512]{1,0:T(8,128)(2,1)S(1)}, u32[]{:S(2)}, u32[]{:S(2)}) collective-permute-start(bf16[128,512]{1,0:T(8,128)(2,1)S(1)} %fusion.4.refs_0_), channel_id=1, source_target_pairs={{0,12},{4,0},{8,4},{12,8},{1,13},{5,1},{9,5},{13,9},{2,14},{6,2},{... | collective-permute-start | bytes 393224 | tf_op jit(solution)/shard_map/ppermute | solution.py:316
  19.5 7.7 %collective-permute-start.4 = (bf16[128,512]{1,0:T(8,128)(2,1)S(1)}, bf16[128,512]{1,0:T(8,128)(2,1)S(1)}, u32[]{:S(2)}, u32[]{:S(2)}) collective-permute-start(bf16[128,512]{1,0:T(8,128)(2,1)S(1)} %fusion.4.refs_0_), channel_id=1, source_target_pairs={{0,8},{4,12},{8,0},{12,4},{1,9},{5,13},{9,1},{13,5},{2,10},{6,14},... | collective-permute-start | bytes 393224 | tf_op jit(solution)/shard_map/ppermute | solution.py:316
  19.5 11.0 %collective-permute-start.3 = (bf16[128,512]{1,0:T(8,128)(2,1)S(1)}, bf16[128,512]{1,0:T(8,128)(2,1)S(1)}, u32[]{:S(2)}, u32[]{:S(2)}) collective-permute-start(bf16[128,512]{1,0:T(8,128)(2,1)S(1)} %fusion.4.refs_0_), channel_id=1, source_target_pairs={{0,4},{4,8},{8,12},{12,0},{1,5},{5,9},{9,13},{13,1},{2,6},{6,10},{... | collective-permute-start | bytes 393224 | tf_op jit(solution)/shard_map/ppermute | solution.py:316
  30.5 32.9 %collective-permute-start.6 = (bf16[2,512,128]{2,1,0:T(8,128)(2,1)S(1)}, bf16[2,512,128]{2,1,0:T(8,128)(2,1)S(1)}, u32[]{:S(2)}, u32[]{:S(2)}) collective-permute-start(bf16[2,512,128]{2,1,0:T(8,128)(2,1)S(1)} %get-tuple-element.38), channel_id=1, source_target_pairs={{0,4},{4,8},{8,12},{1,5},{5,9},{9,13},{2,6},{6,10},{10,14},{3,7},{... | collective-permute-start | bytes 786440 | tf_op jit(solution)/shard_map/ppermute | solution.py:348
  34.6 28.8 %collective-permute-start.7 = (bf16[2,512,128]{2,1,0:T(8,128)(2,1)S(1)}, bf16[2,512,128]{2,1,0:T(8,128)(2,1)S(1)}, u32[]{:S(2)}, u32[]{:S(2)}) collective-permute-start(bf16[2,512,128]{2,1,0:T(8,128)(2,1)S(1)} %get-tuple-element.39), channel_id=1, source_target_pairs={{4,0},{8,4},{12,8},{5,1},{9,5},{13,9},{6,2},{10,6},{14,10},{7,3},{... | collective-permute-start | bytes 786440 | tf_op jit(solution)/shard_map/ppermute | solution.py:349
  46.8 4.9 %collective-permute-start.10 = (bf16[128,640]{1,0:T(8,128)(2,1)S(1)}, bf16[128,640]{1,0:T(8,128)(2,1)S(1)}, u32[]{:S(2)}, u32[]{:S(2)}) collective-permute-start(bf16[128,640]{1,0:T(8,128)(2,1)S(1)} %get-tuple-element.75), channel_id=1, source_target_pairs={{0,12},{4,0},{8,4},{12,8},{1,13},{5,1},{9,5},{13,9},{2,14},{6,2},{... | collective-permute-start | bytes 491528 | tf_op jit(solution)/shard_map/ppermute | solution.py:316
  46.8 13.0 %collective-permute-start.9 = (bf16[128,640]{1,0:T(8,128)(2,1)S(1)}, bf16[128,640]{1,0:T(8,128)(2,1)S(1)}, u32[]{:S(2)}, u32[]{:S(2)}) collective-permute-start(bf16[128,640]{1,0:T(8,128)(2,1)S(1)} %get-tuple-element.76), channel_id=1, source_target_pairs={{0,8},{4,12},{8,0},{12,4},{1,9},{5,13},{9,1},{13,5},{2,10},{6,14},... | collective-permute-start | bytes 491528 | tf_op jit(solution)/shard_map/ppermute | solution.py:316
  49.5 13.9 %collective-permute-start.8 = (bf16[128,640]{1,0:T(8,128)(2,1)S(1)}, bf16[128,640]{1,0:T(8,128)(2,1)S(1)}, u32[]{:S(2)}, u32[]{:S(2)}) collective-permute-start(bf16[128,640]{1,0:T(8,128)(2,1)S(1)} %get-tuple-element.77), channel_id=1, source_target_pairs={{0,4},{4,8},{8,12},{12,0},{1,5},{5,9},{9,13},{13,1},{2,6},{6,10},{... | collective-permute-start | bytes 491528 | tf_op jit(solution)/shard_map/ppermute | solution.py:316
  51.7 28.7 %copy-start.3 = (bf16[1024,512]{1,0:T(8,128)(2,1)S(1)}, bf16[1024,512]{1,0:T(8,128)(2,1)}, u32[]{:S(2)}) copy-start(bf16[1024,512]{1,0:T(8,128)(2,1)} %q_ref.5) | copy-start | bytes 3145732
  51.7 28.7 %copy-start.4 = (s32[8]{0:T(128)S(1)}, s32[8]{0:T(128)}, u32[]{:S(2)}) copy-start(s32[8]{0:T(128)} %radius_ref.1) | copy-start | bytes 100
  51.7 12.4 %copy-start.6 = (bf16[128,640]{1,0:T(8,128)(2,1)}, bf16[128,640]{1,0:T(8,128)(2,1)S(1)}, u32[]{:S(2)}) copy-start(bf16[128,640]{1,0:T(8,128)(2,1)S(1)} %collective-permute-done.10.refs_3_) | copy-start | bytes 491524
  59.9 4.2 %copy-start.7 = (bf16[128,640]{1,0:T(8,128)(2,1)}, bf16[128,640]{1,0:T(8,128)(2,1)S(1)}, u32[]{:S(2)}) copy-start(bf16[128,640]{1,0:T(8,128)(2,1)S(1)} %collective-permute-done.9.refs_2_) | copy-start | bytes 491524
  63.4 0.7 copy-start.8
  66.7 10.4 %copy-start.5 = (bf16[128,512]{1,0:T(8,128)(2,1)S(1)}, bf16[128,512]{1,0:T(8,128)(2,1)}, u32[]{:S(2)}) copy-start(bf16[128,512]{1,0:T(8,128)(2,1)} %combine.1) | copy-start | bytes 393220
  66.7 29.7 %collective-permute-start.14 = (bf16[2,512,384]{2,1,0:T(8,128)(2,1)}, bf16[2,512,384]{2,1,0:T(8,128)(2,1)S(1)}, u32[]{:S(2)}, u32[]{:S(2)}) collective-permute-start(bf16[2,512,384]{2,1,0:T(8,128)(2,1)} %get-tuple-element.59), channel_id=1, source_target_pairs={{0,4},{4,8},{8,12},{1,5},{5,9},{9,13},{2,6},{6,10},{10,14},{3,7},{... | collective-permute-start | bytes 2359304 | tf_op jit(solution)/shard_map/ppermute | solution.py:348
  70.9 25.4 %collective-permute-start.15 = (bf16[2,512,384]{2,1,0:T(8,128)(2,1)}, bf16[2,512,384]{2,1,0:T(8,128)(2,1)S(1)}, u32[]{:S(2)}, u32[]{:S(2)}) collective-permute-start(bf16[2,512,384]{2,1,0:T(8,128)(2,1)} %get-tuple-element.60), channel_id=1, source_target_pairs={{4,0},{8,4},{12,8},{5,1},{9,5},{13,9},{6,2},{10,6},{14,10},{7,3},{... | collective-permute-start | bytes 2359304 | tf_op jit(solution)/shard_map/ppermute | solution.py:349
  77.1 13.7 %collective-permute-start.13 = (bf16[128,512]{1,0:T(8,128)(2,1)S(1)}, bf16[128,512]{1,0:T(8,128)(2,1)S(1)}, u32[]{:S(2)}, u32[]{:S(2)}) collective-permute-start(bf16[128,512]{1,0:T(8,128)(2,1)S(1)} %copy-done.5), channel_id=1, source_target_pairs={{0,3},{1,0},{2,1},{3,2},{4,7},{5,4},{6,5},{7,6},{8,11},{9,8},{10,9... | collective-permute-start | bytes 393224 | tf_op jit(solution)/shard_map/ppermute | solution.py:316
  77.9 12.9 %collective-permute-start.12 = (bf16[128,512]{1,0:T(8,128)(2,1)S(1)}, bf16[128,512]{1,0:T(8,128)(2,1)S(1)}, u32[]{:S(2)}, u32[]{:S(2)}) collective-permute-start(bf16[128,512]{1,0:T(8,128)(2,1)S(1)} %copy-done.5), channel_id=1, source_target_pairs={{0,2},{1,3},{2,0},{3,1},{4,6},{5,7},{6,4},{7,5},{8,10},{9,11},{10,... | collective-permute-start | bytes 393224 | tf_op jit(solution)/shard_map/ppermute | solution.py:316
  79.1 11.6 %collective-permute-start.11 = (bf16[128,512]{1,0:T(8,128)(2,1)S(1)}, bf16[128,512]{1,0:T(8,128)(2,1)S(1)}, u32[]{:S(2)}, u32[]{:S(2)}) collective-permute-start(bf16[128,512]{1,0:T(8,128)(2,1)S(1)} %copy-done.5), channel_id=1, source_target_pairs={{0,1},{1,2},{2,3},{3,0},{4,5},{5,6},{6,7},{7,4},{8,9},{9,10},{10,1... | collective-permute-start | bytes 393224 | tf_op jit(solution)/shard_map/ppermute | solution.py:316
  80.4 10.5 %copy-start.1 = (bf16[2,2048,512]{2,1,0:T(8,128)(2,1)S(1)}, bf16[2,2048,512]{2,1,0:T(8,128)(2,1)}, u32[]{:S(2)}) copy-start(bf16[2,2048,512]{2,1,0:T(8,128)(2,1)} %proj_ref.1) | copy-start | bytes 12582916
  93.1 30.8 %collective-permute-start.18 = (bf16[2,128,512]{2,1,0:T(8,128)(2,1)S(1)}, bf16[2,128,512]{2,1,0:T(8,128)(2,1)S(1)}, u32[]{:S(2)}, u32[]{:S(2)}) collective-permute-start(bf16[2,128,512]{2,1,0:T(8,128)(2,1)S(1)} %project.1.refs_0_), channel_id=1, source_target_pairs={{0,12},{4,0},{8,4},{12,8},{1,13},{5,1},{9,5},{13,9},{2,14},{6,2},{... | collective-permute-start | bytes 786440 | tf_op jit(solution)/shard_map/ppermute | solution.py:316
  93.1 30.7 %collective-permute-start.17 = (bf16[2,128,512]{2,1,0:T(8,128)(2,1)S(1)}, bf16[2,128,512]{2,1,0:T(8,128)(2,1)S(1)}, u32[]{:S(2)}, u32[]{:S(2)}) collective-permute-start(bf16[2,128,512]{2,1,0:T(8,128)(2,1)S(1)} %project.1.refs_0_), channel_id=1, source_target_pairs={{0,8},{4,12},{8,0},{12,4},{1,9},{5,13},{9,1},{13,5},{2,10},{6,14},... | collective-permute-start | bytes 786440 | tf_op jit(solution)/shard_map/ppermute | solution.py:316
  95.2 28.7 %collective-permute-start.16 = (bf16[2,128,512]{2,1,0:T(8,128)(2,1)S(1)}, bf16[2,128,512]{2,1,0:T(8,128)(2,1)S(1)}, u32[]{:S(2)}, u32[]{:S(2)}) collective-permute-start(bf16[2,128,512]{2,1,0:T(8,128)(2,1)S(1)} %project.1.refs_0_), channel_id=1, source_target_pairs={{0,4},{4,8},{8,12},{12,0},{1,5},{5,9},{9,13},{13,1},{2,6},{6,10},{... | collective-permute-start | bytes 786440 | tf_op jit(solution)/shard_map/ppermute | solution.py:316
